TPU v7x, 512 devices: a whole 4x8x8 slice. The times are simulated.
512 devices in a mesh: gx: 16 (over z, core), gy: 16 (over x, y_hi), sub: 2 (over y_lo).
Axes of the slice: x: 4, y: 8 (y_hi: 4, y_lo: 2; y = y_hi * 2 + y_lo), z: 8, core: 2. Of those that a mesh axis runs over, the one named last changes fastest.
Arguments:
- activity: float32 [128, 128, 128], P('gx', 'gy'), may hold values from 0.2 to 2
- anatomy: float32 [128, 128, 128], P('gx', 'gy'), may hold values from 0.2 to 2
- mr_data: float32 [128, 128, 128], P('gx', 'gy'), may hold values from 0.2 to 2
- sensitivity: float32 [128, 128, 128], P('gx', 'gy'), may hold values from 0.25 to 1
- blocks: bfloat16 [12288, 6, 128, 128], P(('gx', 'gy', 'sub')), may hold values from 9.9658966e-05 to 0.0025939941
- brick_ids: int32 [12288, 6], P(('gx', 'gy', 'sub')), may hold values from 0 to 1023, as said below
- counts: float32 [12288, 128], P(('gx', 'gy', 'sub')), may hold values from 0.2 to 5
- background: float32 [12288, 128], P(('gx', 'gy', 'sub')), may hold values from 0.2 to 1
Outputs:
- activity_next: float32 [128, 128, 128], P('gx', 'gy')
- anatomy_next: float32 [128, 128, 128], P('gx', 'gy')
Inputs may be any that keep to these rules, and one draw needn't show every extreme that they name: `brick_ids`: an entry names a brick of its tile's row, numbered as gy * 64 + (local x * 8 + local y) * 1 + z block. The 6 bricks of one tile lie along a line: the same x and z block, at 6 consecutive values of y.
All inputs are finite; a program needn't handle non-finite values.
Results may differ from a plain program's by a relative error of at most 0.00042.
Values may be sent and summed in bfloat16 or wider, within the bound.
A program may use at most 64 MiB of HBM per device.

v0:
```python
import jax
import jax.numpy as jnp
from jax import lax
from jax.sharding import PartitionSpec as P

ITERS = 2


EPSILON_SQ = 0.01
BETA = 0.2
TAU = 0.5
FLOOR = 0.05


def passed_along(block, axis, distance):
    devices = range(lax.axis_size(axis))
    route = [(i - distance, i) for i in devices if i - distance in devices]
    return lax.ppermute(block, axis, route)


def fluxes(grad_act, grad_ana):
    cross_x = grad_act[1] * grad_ana[2] - grad_act[2] * grad_ana[1]
    cross_y = grad_act[2] * grad_ana[0] - grad_act[0] * grad_ana[2]
    cross_z = grad_act[0] * grad_ana[1] - grad_act[1] * grad_ana[0]
    inverse = 1.0 / jnp.sqrt(EPSILON_SQ + cross_x * cross_x + cross_y * cross_y + cross_z * cross_z)
    norm_act = grad_act[0] * grad_act[0] + grad_act[1] * grad_act[1] + grad_act[2] * grad_act[2]
    norm_ana = grad_ana[0] * grad_ana[0] + grad_ana[1] * grad_ana[1] + grad_ana[2] * grad_ana[2]
    inner = grad_act[0] * grad_ana[0] + grad_act[1] * grad_ana[1] + grad_act[2] * grad_ana[2]
    flux_act = tuple(((norm_ana * grad_act[d] - inner * grad_ana[d]) * inverse for d in range(3)))
    flux_ana = tuple(((norm_act * grad_ana[d] - inner * grad_act[d]) * inverse for d in range(3)))
    return (flux_act, flux_ana)


def along_depth(centre):
    return jnp.concatenate(
        [centre[:, :, 1:] - centre[:, :, :-1], jnp.zeros_like(centre[:, :, :1])], 2
    )


def forward_parts(field, next_x, next_y, spot_x, spot_y, total_x, total_y):
    along_x = jnp.concatenate([field[1:], next_x], 0) - field
    along_y = jnp.concatenate([field[:, 1:], next_y], 1) - field
    along_x = jnp.where(spot_x[:, None, None] < total_x - 1, along_x, 0.0)
    along_y = jnp.where(spot_y[None, :, None] < total_y - 1, along_y, 0.0)
    return (along_x, along_y, along_depth(field))


def lower_step(values):
    return jnp.concatenate([jnp.zeros_like(values[:, :, :1]), values[:, :, :-1]], 2) - values


def prior_terms(current_act, current_ana, start_x, start_y, total_x, total_y):
    size_x, size_y, size_z = current_act.shape
    stacked = jnp.stack([current_act, current_ana])
    next_x = passed_along(stacked[:, 0:1], "gx", -1)
    next_y = passed_along(stacked[:, :, 0:1], "gy", -1)
    spot_x = start_x + jnp.arange(size_x)
    spot_y = start_y + jnp.arange(size_y)
    grad_act = forward_parts(current_act, next_x[0], next_y[0], spot_x, spot_y, total_x, total_y)
    grad_ana = forward_parts(current_ana, next_x[1], next_y[1], spot_x, spot_y, total_x, total_y)
    flux_act, flux_ana = fluxes(grad_act, grad_ana)
    last_x = jnp.stack([flux_act[0][size_x - 1 :], flux_ana[0][size_x - 1 :]])
    last_y = jnp.stack([flux_act[1][:, size_y - 1 :], flux_ana[1][:, size_y - 1 :]])
    prev_x = passed_along(last_x, "gx", 1)
    prev_y = passed_along(last_y, "gy", 1)
    before_act_x = jnp.concatenate([prev_x[0], flux_act[0][:-1]], 0)
    before_ana_x = jnp.concatenate([prev_x[1], flux_ana[0][:-1]], 0)
    before_act_y = jnp.concatenate([prev_y[0], flux_act[1][:, :-1]], 1)
    before_ana_y = jnp.concatenate([prev_y[1], flux_ana[1][:, :-1]], 1)
    prior_act = before_act_x - flux_act[0] + (before_act_y - flux_act[1]) + lower_step(flux_act[2])
    prior_ana = before_ana_x - flux_ana[0] + (before_ana_y - flux_ana[1]) + lower_step(flux_ana[2])
    return (prior_act, prior_ana)


def local(activity, anatomy, mr_data, sensitivity, blocks, brick_ids, counts, background):
    size_x, size_y, size_z = activity.shape
    brick_len = blocks.shape[3]
    brick_count = size_x * size_y * size_z // brick_len
    total_x = size_x * lax.axis_size("gx")
    total_y = size_y * lax.axis_size("gy")
    start_x = lax.axis_index("gx") * size_x
    start_y = lax.axis_index("gy") * size_y
    current_act = activity
    current_ana = anatomy
    flat_ids = brick_ids.reshape(-1)
    for repeat in range(ITERS):
        own_bricks = current_act.astype(jnp.bfloat16).reshape(brick_count, brick_len)
        row_bricks = lax.all_gather(own_bricks, "gy", axis=0, tiled=True)
        picked = row_bricks[brick_ids]
        expected = (
            jnp.einsum("tklj,tkj->tl", blocks, picked, preferred_element_type=jnp.float32)
            + background
        )
        ratios = (1.0 - counts / expected).astype(jnp.bfloat16)
        backward = jnp.einsum("tklj,tl->tkj", blocks, ratios, preferred_element_type=jnp.float32)
        partial_value = jax.ops.segment_sum(
            backward.reshape(-1, brick_len), flat_ids, num_segments=row_bricks.shape[0]
        )
        portion = lax.psum_scatter(partial_value, "gy", scatter_dimension=0, tiled=True)
        summed = lax.psum(portion, "sub")
        data_grad = summed.reshape(size_x, size_y, size_z)
        prior_act, prior_ana = prior_terms(
            current_act, current_ana, start_x, start_y, total_x, total_y
        )
        current_act = jnp.maximum(
            current_act - current_act / sensitivity * (data_grad + BETA * prior_act), FLOOR
        )
        current_ana = current_ana - TAU * (current_ana - mr_data + BETA * prior_ana)
    return (current_act, current_ana)


def solution(mesh):
    in_specs = (
        P("gx", "gy", None),
        P("gx", "gy", None),
        P("gx", "gy", None),
        P("gx", "gy", None),
        P(("gx", "gy", "sub"), None, None, None),
        P(("gx", "gy", "sub"), None),
        P(("gx", "gy", "sub"), None),
        P(("gx", "gy", "sub"), None),
    )
    out_specs = (P("gx", "gy", None), P("gx", "gy", None))
    return jax.shard_map(local, mesh=mesh, in_specs=in_specs, out_specs=out_specs, check_vma=False)
```

profile of v0, /device:TPU:8, one launch (start us, length us, event | category | flops | bytes accessed | tf_op | source)
XLA Modules:
  0.0 334.2 jit_solution(16170323490133602195)
XLA Ops:
  7.2 0.0 reduce-scatter.3.cloned.1.call-start
  7.2 0.8 pad_maximum_fusion
  8.0 1.3 collective-permute-start.1
  9.3 0.7 pad_maximum_fusion.1
  10.0 1.3 collective-permute-start
  11.3 0.8 copy.71
  12.1 0.8 copy.80
  12.8 0.7 compare_select_fusion
  13.5 0.1 copy.70
  13.6 0.1 reshape.42
  13.7 0.1 slice_subtract_fusion.2
  13.9 0.8 slice.168
  14.6 0.8 slice.176
  15.4 0.8 copy.69
  16.1 0.1 reshape.58
  16.3 0.9 subtract_multiply_fusion.5
  17.1 0.9 fusion.55
  18.3 3.0 collective-permute-start.2
  21.4 5.4 %collective-permute-start.3 = (f32[2,8,1,128]{3,1,2,0:T(8,128)S(1)}, f32[2,8,1,128]{3,1,2,0:T(8,128)S(1)}, u32[]{:S(2)}, u32[]{:S(2)}) collective-permute-start(f32[2,8,1,128]{3,1,2,0:T(8,128)S(1)} %pad_maximum_fusion.3), channel_id=1, source_target_pairs={{0,2},{2,4},{4,6},{6,8},{8,10},{10,12},{12,14},{14,16},{16,18},{18... | collective-permute-start | bytes 24584 | tf_op jit(solution)/shard_map/ppermute | solution.py:18
  26.9 43.7 %all_gather.6 = bf16[1024,128]{1,0:T(8,128)(2,1)S(1)} all-gather(bf16[64,128]{1,0:T(8,128)(2,1)S(1)} %get-tuple-element.36), channel_id=1, replica_groups=mesh['gx'=16,'gy'=16,'sub'=2] {'gy'}, dimensions={0}, use_global_device_ids=true | all-gather | bytes 278528 | tf_op jit(solution)/shard_map/all_gather | solution.py:88
  70.5 0.7 gather_fusion
  71.3 3.8 %fusion.67 = f32[24,1,128,1]{2,1,3,0:T(1,128)S(1)} fusion(bf16[24,6,128,1]{2,3,1,0:T(2,128)(2,1)S(1)} %reshape.87, bf16[24,6,128,128]{3,2,1,0:T(8,128)(2,1)} %param.12), kind=kOutput, calls=%fused_computation.140 | convolution fusion | flops 4718592 | bytes 4767744 | tf_op jit(solution)/shard_map/tklj,tkj->tl/dot_general | solution.py:91
  75.1 0.0 copy-done.6
  75.2 0.7 fusion.45
  75.9 1.9 scatter_custom_fusion
  77.8 0.0 reduce-scatter.5.cloned.1.call-start
  78.0 0.1 fusion.16
  78.1 0.1 slice_subtract_fusion.1
  78.2 0.1 fusion.10
  78.2 88.0 %reduce-scatter.3.cloned.1.call-done = f32[64,128]{1,0:T(8,128)} async-done(((f32[1024,128]{1,0:T(8,128)}), f32[64,128]{1,0:T(8,128)}) %reduce-scatter.3.cloned.1.call-update) | async-done | bytes 32784 | tf_op jit(solution)/shard_map/reduce_scatter | solution.py:99
  166.3 8.9 %psum.14 = f32[8,8,128]{2,1,0:T(8,128)S(1)} all-reduce(f32[8,8,128]{2,1,0:T(8,128)} %bitcast.103), channel_id=1, replica_groups=mesh['gx'=16,'gy'=16,'sub'=2] {'sub'}, use_global_device_ids=true, to_apply=%region_2.0 | all-reduce | flops 8192 | bytes 65536 | tf_op jit(solution)/shard_map/psum | solution.py:100
  175.4 0.1 slice_subtract_fusion
  175.4 1.3 collective-permute-start.4
  176.7 1.3 collective-permute-start.5
  178.0 44.6 %all_gather.7 = bf16[1024,128]{1,0:T(8,128)(2,1)S(1)} all-gather(bf16[64,128]{1,0:T(8,128)(2,1)S(1)} %get-tuple-element.11), channel_id=1, replica_groups=mesh['gx'=16,'gy'=16,'sub'=2] {'gy'}, dimensions={0}, use_global_device_ids=true | all-gather | bytes 278528 | tf_op jit(solution)/shard_map/all_gather | solution.py:88
  222.6 0.7 gather_fusion.1
  223.4 3.7 %fusion.68 = f32[24,1,128,1]{2,1,3,0:T(1,128)S(1)} fusion(bf16[24,6,128,1]{2,3,1,0:T(2,128)(2,1)S(1)} %reshape.89, bf16[24,6,128,128]{3,2,1,0:T(8,128)(2,1)} %param.12), kind=kOutput, calls=%fused_computation.141 | convolution fusion | flops 4718592 | bytes 4767744 | tf_op jit(solution)/shard_map/tklj,tkj->tl/dot_general | solution.py:91
  227.1 3.1 fusion.43
  230.2 1.9 scatter_custom_fusion.1
  232.1 0.1 multiply_add_fusion.1
  232.4 1.3 collective-permute-start.6
  233.7 2.0 collective-permute-start.7
  235.8 1.3 collective-permute-done.7
  237.1 0.1 fusion.22
  237.2 0.7 fusion.28
  237.9 79.8 %reduce-scatter.5.cloned.1.call-done = f32[64,128]{1,0:T(8,128)} async-done(((f32[1024,128]{1,0:T(8,128)}), f32[64,128]{1,0:T(8,128)}) %reduce-scatter.5.cloned.1.call-update) | async-done | bytes 32784 | tf_op jit(solution)/shard_map/reduce_scatter | solution.py:99
  317.8 8.9 %psum.15 = f32[8,8,128]{2,1,0:T(8,128)S(1)} all-reduce(f32[8,8,128]{2,1,0:T(8,128)} %bitcast.102), channel_id=1, replica_groups=mesh['gx'=16,'gy'=16,'sub'=2] {'sub'}, use_global_device_ids=true, to_apply=%region_5.6 | all-reduce | flops 8192 | bytes 65536 | tf_op jit(solution)/shard_map/psum | solution.py:100
  326.7 0.6 fusion.32
  (82 shorter events, 0.7 us)
Async XLA Ops:
  7.2 68.0 %copy-start.5 = (f32[24,128]{1,0:T(8,128)S(1)}, f32[24,128]{1,0:T(8,128)}, u32[]{:S(2)}) copy-start(f32[24,128]{1,0:T(8,128)} %param.14) | copy-start | bytes 36868
  7.2 68.0 %copy-start.6 = (f32[24,128]{1,0:T(8,128)S(1)}, f32[24,128]{1,0:T(8,128)}, u32[]{:S(2)}) copy-start(f32[24,128]{1,0:T(8,128)} %param.15) | copy-start | bytes 36868
  7.2 159.1 %reduce-scatter.3.cloned.1.call-start = ((), (), s32[]{:S(2)}) async-start(), calls=%async_computation.2 | async-start | bytes 557056 | tf_op jit(solution)/shard_map/reduce_scatter | solution.py:99
  8.0 8.2 %collective-permute-start.1 = (f32[2,8,1,128]{3,2,1,0:T(1,128)S(1)}, f32[2,8,1,128]{3,2,1,0:T(1,128)S(1)}, u32[]{:S(2)}, u32[]{:S(2)}) collective-permute-start(f32[2,8,1,128]{3,2,1,0:T(1,128)S(1)} %pad_maximum_fusion), channel_id=1, source_target_pairs={{2,0},{4,2},{6,4},{8,6},{10,8},{12,10},{14,12},{16,14},{18,16},{20... | collective-permute-start | bytes 24584 | tf_op jit(solution)/shard_map/ppermute | solution.py:18
  10.0 7.1 %collective-permute-start = (f32[2,1,8,128]{3,2,1,0:T(8,128)S(1)}, f32[2,1,8,128]{3,2,1,0:T(8,128)S(1)}, u32[]{:S(2)}, u32[]{:S(2)}) collective-permute-start(f32[2,1,8,128]{3,2,1,0:T(8,128)S(1)} %pad_maximum_fusion.1), channel_id=1, source_target_pairs={{32,0},{64,32},{96,64},{128,96},{160,128},{192,160},{224,192},{256... | collective-permute-start | bytes 24584 | tf_op jit(solution)/shard_map/ppermute | solution.py:18
  18.3 59.5 %collective-permute-start.2 = (f32[2,1,8,128]{3,2,1,0:T(8,128)S(1)}, f32[2,1,8,128]{3,2,1,0:T(8,128)S(1)}, u32[]{:S(2)}, u32[]{:S(2)}) collective-permute-start(f32[2,1,8,128]{3,2,1,0:T(8,128)S(1)} %pad_maximum_fusion.2), channel_id=1, source_target_pairs={{0,32},{32,64},{64,96},{96,128},{128,160},{160,192},{192,224},{224... | collective-permute-start | bytes 24584 | tf_op jit(solution)/shard_map/ppermute | solution.py:18
  21.4 56.5 %collective-permute-start.3 = (f32[2,8,1,128]{3,1,2,0:T(8,128)S(1)}, f32[2,8,1,128]{3,1,2,0:T(8,128)S(1)}, u32[]{:S(2)}, u32[]{:S(2)}) collective-permute-start(f32[2,8,1,128]{3,1,2,0:T(8,128)S(1)} %pad_maximum_fusion.3), channel_id=1, source_target_pairs={{0,2},{2,4},{4,6},{6,8},{8,10},{10,12},{12,14},{14,16},{16,18},{18... | collective-permute-start | bytes 24584 | tf_op jit(solution)/shard_map/ppermute | solution.py:18
  71.3 3.9 %copy-start = (bf16[24,6,128,128]{3,2,1,0:T(8,128)(2,1)S(1)}, bf16[24,6,128,128]{3,2,1,0:T(8,128)(2,1)}, u32[]{:S(2)}) copy-start(bf16[24,6,128,128]{3,2,1,0:T(8,128)(2,1)} %param.12) | copy-start | bytes 14155780
  71.3 6.6 %copy-start.1 = (f32[8,8,128]{2,1,0:T(8,128)S(1)}, f32[8,8,128]{2,1,0:T(8,128)}, u32[]{:S(2)}) copy-start(f32[8,8,128]{2,1,0:T(8,128)} %param.9) | copy-start | bytes 98308
  71.3 6.6 %copy-start.4 = (f32[8,8,128]{2,1,0:T(8,128)S(1)}, f32[8,8,128]{2,1,0:T(8,128)}, u32[]{:S(2)}) copy-start(f32[8,8,128]{2,1,0:T(8,128)} %param.10) | copy-start | bytes 98308
  75.1 100.1 %copy-start.2 = (f32[8,8,128]{2,1,0:T(8,128)S(1)}, f32[8,8,128]{2,1,0:T(8,128)}, u32[]{:S(2)}) copy-start(f32[8,8,128]{2,1,0:T(8,128)} %param.8) | copy-start | bytes 98308
  75.1 100.1 %copy-start.3 = (f32[8,8,128]{2,1,0:T(8,128)S(1)}, f32[8,8,128]{2,1,0:T(8,128)}, u32[]{:S(2)}) copy-start(f32[8,8,128]{2,1,0:T(8,128)} %param.11) | copy-start | bytes 98308
  77.8 240.0 %reduce-scatter.5.cloned.1.call-start = ((), (), s32[]{:S(2)}) async-start(), calls=%async_computation.3 | async-start | bytes 557056 | tf_op jit(solution)/shard_map/reduce_scatter | solution.py:99
  175.4 56.6 %collective-permute-start.4 = (f32[2,1,8,128]{3,1,2,0:T(1,128)S(1)}, f32[2,1,8,128]{3,1,2,0:T(1,128)S(1)}, u32[]{:S(2)}, u32[]{:S(2)}) collective-permute-start(f32[2,1,8,128]{3,1,2,0:T(1,128)S(1)} %slice.253), channel_id=1, source_target_pairs={{32,0},{64,32},{96,64},{128,96},{160,128},{192,160},{224,192},{256... | collective-permute-start | bytes 24584 | tf_op jit(solution)/shard_map/ppermute | solution.py:18
  176.7 55.4 %collective-permute-start.5 = (f32[2,8,1,128]{3,1,2,0:T(8,128)S(1)}, f32[2,8,1,128]{3,1,2,0:T(8,128)S(1)}, u32[]{:S(2)}, u32[]{:S(2)}) collective-permute-start(f32[2,8,1,128]{3,1,2,0:T(8,128)S(1)} %slice.256), channel_id=1, source_target_pairs={{2,0},{4,2},{6,4},{8,6},{10,8},{12,10},{14,12},{16,14},{18,16},{20... | collective-permute-start | bytes 24584 | tf_op jit(solution)/shard_map/ppermute | solution.py:18
  232.4 3.4 %collective-permute-start.6 = (f32[2,1,8,128]{3,2,1,0:T(8,128)S(1)}, f32[2,1,8,128]{3,2,1,0:T(8,128)S(1)}, u32[]{:S(2)}, u32[]{:S(2)}) collective-permute-start(f32[2,1,8,128]{3,2,1,0:T(8,128)S(1)} %pad_maximum_fusion.4), channel_id=1, source_target_pairs={{0,32},{32,64},{64,96},{96,128},{128,160},{160,192},{192,224},{224... | collective-permute-start | bytes 24584 | tf_op jit(solution)/shard_map/ppermute | solution.py:18
  233.7 3.4 %collective-permute-start.7 = (f32[2,8,1,128]{3,1,2,0:T(8,128)S(1)}, f32[2,8,1,128]{3,1,2,0:T(8,128)S(1)}, u32[]{:S(2)}, u32[]{:S(2)}) collective-permute-start(f32[2,8,1,128]{3,1,2,0:T(8,128)S(1)} %pad_maximum_fusion.5), channel_id=1, source_target_pairs={{0,2},{2,4},{4,6},{6,8},{8,10},{10,12},{12,14},{14,16},{16,18},{18... | collective-permute-start | bytes 24584 | tf_op jit(solution)/shard_map/ppermute | solution.py:18
Sparse Core Ops, SparseCore 0:
  77.9 88.2 reduce-scatter.2
  232.2 85.5 reduce-scatter.4
where the time goes:
time: 335 us; the launch traced here: 334 us
  waiting for transfers between devices  169 us (50%)
  blocking collectives  106 us (32%)
  starting transfers between devices  17 us (5%)
  between operations  14.7 us (4%)
  matrix products  11.2 us (3%)
  other arithmetic  10 us (3%)
  local copies, waits for them, and re-layouts  5.82 us (2%)
    reduce_scatter x2, waiting for transfers between devices, local(): lax.psum_scatter(partial_value, 'gy', scatter_dimension=0, tiled=True)  168 us
    all_gather x2, blocking collectives, local(): row_bricks = lax.all_gather(own_bricks, 'gy', axis=0, tiled=True)  88.3 us
    psum x2, blocking collectives, local(): summed = lax.psum(portion, 'sub')  17.9 us
    ppermute x8, starting transfers between devices, passed_along(): return lax.ppermute(block, axis, route)  16.9 us
    dot_general x2, matrix products, local(): jnp.einsum('tklj,tkj->tl', blocks, picked, preferred_element_type=jnp.flo...  7.46 us
  transfers between devices with their start and end apart: 10, of which 3 were waited for; matrix products, arithmetic and copies ran while one was open for 7% of the time, Pallas kernels for 0%

commit v1 on v0

v1 whole, which is shorter than its diff:
```python
import functools
import math

import jax
import jax.numpy as jnp
from jax import lax
from jax.experimental import pallas as pl
from jax.experimental.pallas import tpu as pltpu
from jax.sharding import PartitionSpec as P

ITERS = 2
EPSILON_SQ = 0.01
BETA = 0.2
TAU = 0.5
FLOOR = 0.05

MESH = pl.DeviceIdType.MESH
F32 = jnp.float32
BF16 = jnp.bfloat16

NCX, NCY = 4, 8
NGX, NGY = 16, 16
SLABS = 2 * NGX
TILES, K, LORT, BRICK = 24, 6, 128, 128
KP = 8
ENTRIES = TILES * KP
ENTRIES_PAD = 256
HALF = 32
QUAD = NCY * HALF

CODE_EPS = 1.0 / 64.0
CODE_MAX = 256.0
CODE_Q = 32766.0 / math.log1p(CODE_MAX / CODE_EPS)


def around(value, size):
    return lax.rem(value + size, size)


def offsets():
    every = [(a, b) for a in range(NCX) for b in range(NCY) if (a, b) != (0, 0)]
    return sorted(every, key=lambda p: -(min(p[0], NCX - p[0]) + min(p[1], NCY - p[1])))


OFFSETS = offsets()
INDEX = {p: i for i, p in enumerate(OFFSETS)}
NEAR_FIRST = OFFSETS[::-1]


def encode(x):
    code = jnp.log(1.0 + jnp.abs(x) * (1.0 / CODE_EPS)) * CODE_Q + 0.5
    code = jnp.minimum(code, 32767.0)
    return jnp.where(x < 0.0, -code, code).astype(jnp.int32).astype(jnp.int16)


def decode(code):
    value = code.astype(jnp.int32).astype(F32)
    size = (jnp.exp(jnp.abs(value) * (1.0 / CODE_Q)) - 1.0) * CODE_EPS
    return jnp.where(value < 0.0, -size, size)


def flux(gu, gv):
    cross_x = gu[1] * gv[2] - gu[2] * gv[1]
    cross_y = gu[2] * gv[0] - gu[0] * gv[2]
    cross_z = gu[0] * gv[1] - gu[1] * gv[0]
    inverse = 1.0 / jnp.sqrt(EPSILON_SQ + cross_x * cross_x + cross_y * cross_y + cross_z * cross_z)
    norm_u = gu[0] * gu[0] + gu[1] * gu[1] + gu[2] * gu[2]
    norm_v = gv[0] * gv[0] + gv[1] * gv[1] + gv[2] * gv[2]
    inner = gu[0] * gv[0] + gu[1] * gv[1] + gu[2] * gv[2]
    flux_u = [(norm_v * gu[d] - inner * gv[d]) * inverse for d in range(3)]
    flux_v = [(norm_u * gv[d] - inner * gu[d]) * inverse for d in range(3)]
    return flux_u, flux_v


def dot(a, b, dims):
    return lax.dot_general(a, b, (dims, ((), ())), preferred_element_type=F32)


NN = ((1,), (0,))
NT = ((1,), (1,))


def kernel(
    act_hbm, ana_hbm, mr_hbm, sens_hbm, blocks_hbm, ids_hbm, counts_hbm, back_hbm,
    u_out, v_out,
    u_ref, v_ref, mr_ref, sens_ref, blk, ids_ref, counts_ref, back_ref,
    gather_ref, scatter_ref, full, picked, expect, ratio, back_terms, own_part,
    send_b, recv_b, send_h, recv_h, strip,
    load_sem, a_send, a_recv, b_send, b_recv, h_send, h_recv, c_send, c_recv,
):
    gx = lax.axis_index("gx")
    gy = lax.axis_index("gy")
    sub = lax.axis_index("sub")
    cx, cy = gy // 4, (gy % 4) * 2 + sub
    slab = gx * 2 + sub

    def peer(a, b):
        x, y = lax.rem(cx + a, NCX), lax.rem(cy + b, NCY)
        return (gx, x * 4 + y // 2, lax.rem(y, 2))

    def neighbour(ds, dg):
        other = around(slab + ds, SLABS)
        return (other // 2, around(gy + dg, NGY), lax.rem(other, 2))

    barrier = pltpu.get_barrier_semaphore()
    side = 2 * sub - 1
    for a, b in OFFSETS:
        pl.semaphore_signal(barrier, inc=1, device_id=peer(a, b), device_id_type=MESH)
    pl.semaphore_signal(barrier, inc=1, device_id=neighbour(side, 0), device_id_type=MESH)
    pl.semaphore_signal(barrier, inc=1, device_id=neighbour(side, -side), device_id_type=MESH)

    mine = pl.ds(sub * 4, 4)
    loads = [
        pltpu.make_async_copy(act_hbm.at[mine], u_ref, load_sem.at[0]),
        pltpu.make_async_copy(ana_hbm.at[mine], v_ref, load_sem.at[1]),
        pltpu.make_async_copy(ids_hbm, ids_ref, load_sem.at[2]),
        pltpu.make_async_copy(blocks_hbm, blk, load_sem.at[3]),
        pltpu.make_async_copy(counts_hbm, counts_ref, load_sem.at[4]),
        pltpu.make_async_copy(back_hbm, back_ref, load_sem.at[5]),
        pltpu.make_async_copy(mr_hbm.at[mine], mr_ref, load_sem.at[6]),
        pltpu.make_async_copy(sens_hbm.at[mine], sens_ref, load_sem.at[7]),
    ]
    for load in loads:
        load.start()

    own_rows = pl.ds(pl.multiple_of(cy * HALF, HALF), HALF)
    row_id = lax.broadcasted_iota(jnp.int32, (8, BRICK), 0)
    lane_id = lax.broadcasted_iota(jnp.int32, (8, BRICK), 1)

    def share(phase):
        copies = []
        for a, b in OFFSETS:
            i = INDEX[a, b]
            copies.append(pltpu.make_async_remote_copy(
                src_ref=full.at[phase, 0, own_rows], dst_ref=full.at[phase, a, own_rows],
                send_sem=a_send.at[phase, i], recv_sem=a_recv.at[phase, i],
                device_id=peer(a, b), device_id_type=MESH))
        for copy in copies:
            copy.start()
        return copies

    def pack_halo(phase):
        for f, ref in enumerate((u_ref, v_ref)):
            send_h[phase, 0, f] = ref[0]
            send_h[phase, 1, f] = ref[3]
            for x in range(4):
                send_h[phase, 2, f, x:x + 1, :] = ref[x, 0:1, :]
                send_h[phase, 3, f, x:x + 1, :] = ref[x, 7:8, :]
            send_h[phase, 4, f, 0:1, :] = ref[3, 0:1, :]
            send_h[phase, 5, f, 0:1, :] = ref[0, 7:8, :]

    def share_halo(phase):
        copies = []
        for i, (ds, dg) in enumerate(((-1, 0), (1, 0), (0, -1), (0, 1), (1, -1), (-1, 1))):
            copies.append(pltpu.make_async_remote_copy(
                src_ref=send_h.at[phase, i], dst_ref=recv_h.at[phase, i],
                send_sem=h_send.at[phase, i], recv_sem=h_recv.at[phase, i],
                device_id=neighbour(ds, dg), device_id_type=MESH))
        for copy in copies:
            copy.start()
        return copies

    def gather_bricks(phase, copies):
        total = None
        for a in (0, 1, 3, 2):
            for b in range(NCY):
                if (a, b) != (0, 0):
                    copies[INDEX[a, b]].wait_recv()
            part = dot(gather_ref[a], full[phase, a], NN)
            total = part if total is None else total + part
        picked[...] = total.reshape(TILES, KP, BRICK)

    def only_row(values, k):
        return jnp.where(row_id == k, values, 0.0).astype(BF16)

    def project(step, carry):
        for sub_step in range(4):
            t = step * 4 + sub_step
            x = picked[t]
            total = None
            lhs = jnp.concatenate([only_row(x, k) for k in range(K)], axis=1)
            rhs = jnp.concatenate([blk[t, k] for k in range(K)], axis=1)
            total = dot(lhs, rhs, NT)
            expect[pl.ds(t, 1), :] = jnp.sum(total, axis=0, keepdims=True)
        return carry

    def backproject(step, carry):
        for sub_step in range(4):
            t = step * 4 + sub_step
            r = jnp.broadcast_to(ratio[pl.ds(t, 1), :], (8, LORT))
            lhs = jnp.concatenate([only_row(r, k) for k in range(K)], axis=1)
            back_terms[t] = dot(lhs, blk[t].reshape(K * LORT, BRICK), NN)
        return carry

    def scatter_and_send(phase):
        terms = back_terms[...].reshape(ENTRIES_PAD, BRICK)
        high = terms.astype(BF16)
        low = (terms - high.astype(F32)).astype(BF16)
        copies = [None] * len(OFFSETS)
        for a in (2, 1, 3, 0):
            part = dot(scatter_ref[a], high, NN) + dot(scatter_ref[a], low, NN)
            send_b[phase, a] = encode(part)
            if a == 0:
                own_part[...] = part
            for x, b in OFFSETS:
                if x != a:
                    continue
                i = INDEX[a, b]
                rows = pl.ds(pl.multiple_of(lax.rem(cy + b, NCY) * HALF, HALF), HALF)
                copies[i] = pltpu.make_async_remote_copy(
                    src_ref=send_b.at[phase, a, rows], dst_ref=recv_b.at[phase, i],
                    send_sem=b_send.at[phase, i], recv_sem=b_recv.at[phase, i],
                    device_id=peer(a, b), device_id_type=MESH)
                copies[i].start()
        return copies

    def summed_gradient(phase, copies):
        total = own_part[own_rows, :]
        for p in NEAR_FIRST:
            i = INDEX[p]
            copies[i].wait_recv()
            total = total + decode(recv_b[phase, i])
        return total.reshape(4, 8, BRICK)

    first_slab, last_slab = slab == 0, slab == SLABS - 1
    first_gy, last_gy = gy == 0, gy == NGY - 1

    def prior(phase, copies):
        for copy in copies:
            copy.wait_recv()

        def layers(f, ref):
            return [recv_h[phase, 1, f]] + [ref[x] for x in range(4)] + [recv_h[phase, 0, f]]

        def depth(f):
            return jnp.where(lane_id < BRICK - 1, pltpu.roll(f, BRICK - 1, 1) - f, 0.0)

        def gradient(all_layers, f, x):
            here, after = all_layers[x], all_layers[x + 1]
            along_x = after - here
            if x == 4:
                along_x = jnp.where(last_slab, 0.0, along_x)
            row = recv_h[phase, 4, f, 0:1, :] if x == 0 else recv_h[phase, 2, f, x - 1:x, :]
            shifted = jnp.where(row_id < 7, pltpu.roll(here, 7, 0), jnp.broadcast_to(row, (8, BRICK)))
            along_y = jnp.where(jnp.logical_and(last_gy, row_id == 7), 0.0, shifted - here)
            return along_x, along_y, depth(here)

        def before_gradient(f):
            here = recv_h[phase, 3, f]
            after = recv_h[phase, 5, f, 0:1, :]
            shifted = jnp.where(row_id < 3, pltpu.roll(here, 7, 0), jnp.broadcast_to(after, (8, BRICK)))
            along_x = jnp.where(jnp.logical_and(last_slab, row_id == 3), 0.0, shifted - here)
            return along_x, send_h[phase, 2, f] - here, depth(here)

        us, vs = layers(0, u_ref), layers(1, v_ref)
        parts = [flux(gradient(us, 0, x), gradient(vs, 1, x)) for x in range(5)]
        before = flux(before_gradient(0), before_gradient(1))
        result = []
        for f in range(2):
            strip[f] = before[f][1]
            found = []
            for x in range(1, 5):
                now = parts[x][f]
                prev_x = parts[x - 1][f][0]
                if x == 1:
                    prev_x = jnp.where(first_slab, 0.0, prev_x)
                row = jnp.broadcast_to(strip[f, x - 1:x, :], (8, BRICK))
                row = jnp.where(first_gy, 0.0, row)
                prev_y = jnp.where(row_id > 0, pltpu.roll(now[1], 1, 0), row)
                prev_z = jnp.where(lane_id > 0, pltpu.roll(now[2], 1, 1), 0.0)
                found.append((prev_x - now[0]) + (prev_y - now[1]) + (prev_z - now[2]))
            result.append(found)
        return result

    loads[2].wait()
    ids = ids_ref[...]
    lane6 = lax.broadcasted_iota(jnp.int32, (TILES, KP, K), 2)
    k_of = lax.broadcasted_iota(jnp.int32, (TILES, KP, K), 1)
    spread = jnp.where(lane6 == k_of, jnp.broadcast_to(ids.reshape(TILES, 1, K), (TILES, KP, K)) + 1, 0)
    column = jnp.sum(spread.astype(F32), axis=2, keepdims=True) - 1.0
    column = column.astype(jnp.int32)
    entry = (lax.broadcasted_iota(jnp.int32, (TILES, KP, ENTRIES_PAD), 0) * KP
             + lax.broadcasted_iota(jnp.int32, (TILES, KP, ENTRIES_PAD), 1))
    lanes = lax.broadcasted_iota(jnp.int32, (TILES, KP, ENTRIES_PAD), 2)
    as_row = jnp.where(entry == lanes, column + 1, 0).astype(F32)
    as_row = jnp.sum(jnp.sum(as_row, axis=0), axis=0, keepdims=True).astype(jnp.int32) - 1
    bricks = lax.broadcasted_iota(jnp.int32, (QUAD, ENTRIES_PAD), 0)
    for a in range(NCX):
        came_from = around(cx - a, NCX) * QUAD
        goes_to = lax.rem(cx + a, NCX) * QUAD
        gather_ref[a] = jnp.where(lanes + came_from == column, 1.0, 0.0).reshape(ENTRIES, QUAD).astype(BF16)
        scatter_ref[a] = jnp.where(bricks + goes_to == as_row, 1.0, 0.0).astype(BF16)
    back_terms[pl.ds(TILES, ENTRIES_PAD // KP - TILES)] = jnp.zeros((ENTRIES_PAD // KP - TILES, KP, BRICK), F32)
    send_h[...] = jnp.zeros_like(send_h)
    loads[0].wait()
    loads[1].wait()
    full[0, 0, own_rows, :] = u_ref[...].reshape(HALF, BRICK).astype(BF16)
    pack_halo(0)

    pl.semaphore_wait(barrier, len(OFFSETS) + 2)

    pending = []
    for phase in range(ITERS):
        shared = share(phase)
        halo = share_halo(phase)
        pending += shared + halo
        if phase == 0:
            for i in (3, 4, 5, 6, 7):
                loads[i].wait()
        gather_bricks(phase, shared)
        lax.fori_loop(0, TILES // 4, project, 0)
        ratio[...] = 1.0 - counts_ref[...] / (expect[...] + back_ref[...])
        lax.fori_loop(0, TILES // 4, backproject, 0)
        sent = scatter_and_send(phase)
        pending += sent
        prior_u, prior_v = prior(phase, halo)
        gradient = summed_gradient(phase, sent)
        last = phase == ITERS - 1
        for x in range(4):
            u, v = u_ref[x], v_ref[x]
            new_u = jnp.maximum(u - u / sens_ref[x] * (gradient[x] + BETA * prior_u[x]), FLOOR)
            new_v = v - TAU * (v - mr_ref[x] + BETA * prior_v[x])
            if last:
                u_out[sub * 4 + x] = new_u
                v_out[sub * 4 + x] = new_v
            else:
                u_ref[x] = new_u
                v_ref[x] = new_v
        if not last:
            full[phase + 1, 0, own_rows, :] = u_ref[...].reshape(HALF, BRICK).astype(BF16)
            pack_halo(phase + 1)

    partner = (gx, gy, 1 - sub)
    for i, out in enumerate((u_out, v_out)):
        copy = pltpu.make_async_remote_copy(
            src_ref=out.at[mine], dst_ref=out.at[mine],
            send_sem=c_send.at[i], recv_sem=c_recv.at[i], device_id=partner, device_id_type=MESH)
        copy.start()
        pending.append(copy)
    pending[-1].wait_recv()
    pending[-2].wait_recv()
    for copy in pending:
        copy.wait_send()


def local(activity, anatomy, mr_data, sensitivity, blocks, brick_ids, counts, background):
    n = len(OFFSETS)
    any_space = pl.BlockSpec(memory_space=pl.ANY)
    vmem = pl.BlockSpec(memory_space=pltpu.VMEM)
    half = (4, 8, BRICK)
    dma = pltpu.SemaphoreType.DMA
    return pl.pallas_call(
        kernel,
        out_shape=(jax.ShapeDtypeStruct(activity.shape, F32), jax.ShapeDtypeStruct(anatomy.shape, F32)),
        in_specs=[any_space] * 8,
        out_specs=(vmem, vmem),
        scratch_shapes=[
            pltpu.VMEM(half, F32), pltpu.VMEM(half, F32), pltpu.VMEM(half, F32), pltpu.VMEM(half, F32),
            pltpu.VMEM(blocks.shape, BF16),
            pltpu.VMEM(brick_ids.shape, jnp.int32),
            pltpu.VMEM(counts.shape, F32), pltpu.VMEM(background.shape, F32),
            pltpu.VMEM((NCX, ENTRIES, QUAD), BF16),
            pltpu.VMEM((NCX, QUAD, ENTRIES_PAD), BF16),
            pltpu.VMEM((ITERS, NCX, QUAD, BRICK), BF16),
            pltpu.VMEM((TILES, KP, BRICK), F32),
            pltpu.VMEM((TILES, LORT), F32),
            pltpu.VMEM((TILES, LORT), F32),
            pltpu.VMEM((ENTRIES_PAD // KP, KP, BRICK), F32),
            pltpu.VMEM((QUAD, BRICK), F32),
            pltpu.VMEM((ITERS, NCX, QUAD, BRICK), jnp.int16),
            pltpu.VMEM((ITERS, n, HALF, BRICK), jnp.int16),
            pltpu.VMEM((ITERS, 6, 2, 8, BRICK), F32),
            pltpu.VMEM((ITERS, 6, 2, 8, BRICK), F32),
            pltpu.VMEM((2, 8, BRICK), F32),
            dma((8,)), dma((ITERS, n)), dma((ITERS, n)), dma((ITERS, n)), dma((ITERS, n)),
            dma((ITERS, 6)), dma((ITERS, 6)), dma((2,)), dma((2,)),
        ],
        compiler_params=pltpu.CompilerParams(
            collective_id=0, has_side_effects=True, vmem_limit_bytes=24 * 1024 * 1024),
    )(activity, anatomy, mr_data, sensitivity, blocks, brick_ids, counts, background)


def solution(mesh):
    image = P("gx", "gy", None)
    tiles = ("gx", "gy", "sub")
    in_specs = (image, image, image, image, P(tiles, None, None, None), P(tiles, None), P(tiles, None), P(tiles, None))
    return jax.shard_map(local, mesh=mesh, in_specs=in_specs, out_specs=(image, image), check_vma=False)
```

time: 335 us -> 67.6 us (0.20)
  the two profiles are of different devices: /device:TPU:8 before, /device:TPU:192 now
where the time goes in v1:
time: 67.6 us; the launch traced here: 67.1 us
  Pallas kernels  57.6 us (85%)
  local copies, waits for them, and re-layouts  8.78 us (13%)
    pallas_call x1, Pallas kernels, local(): pl.pallas_call(kernel, out_shape=(jax.ShapeDtypeStruct(activity.shape, F3...  57.6 us
    unnamed x17, local copies, waits for them, and re-layouts  8.78 us

profile of v1, /device:TPU:192, one launch (start us, length us, event | category | flops | bytes accessed | tf_op | source)
XLA Modules:
  0.0 67.1 jit_solution(14779757611114197278)
XLA Ops:
  0.6 0.8 %copy.10.ids_hbm = s32[24,6]{1,0:T(8,128)S(1)} copy(s32[24,6]{0,1:T(8,128)} %param.13) | data formatting | bytes 1152 | tf_op args[5]
  1.4 0.0 copy-start
  1.4 2.3 %copy-done = bf16[24,6,128,128]{3,2,1,0:T(8,128)(2,1)S(1)} copy-done((bf16[24,6,128,128]{3,2,1,0:T(8,128)(2,1)S(1)}, bf16[24,6,128,128]{3,2,1,0:T(8,128)(2,1)}, u32[]{:S(2)}) %copy-start) | copy-done | bytes 4718616
  3.7 0.0 copy-start.1
  3.7 0.8 %copy-done.1 = f32[8,8,128]{2,1,0:T(8,128)S(1)} copy-done((f32[8,8,128]{2,1,0:T(8,128)S(1)}, f32[8,8,128]{2,1,0:T(8,128)}, u32[]{:S(2)}) %copy-start.1) | copy-done | bytes 32792
  4.5 0.0 copy-start.2
  4.5 0.8 %copy-done.2 = f32[8,8,128]{2,1,0:T(8,128)S(1)} copy-done((f32[8,8,128]{2,1,0:T(8,128)S(1)}, f32[8,8,128]{2,1,0:T(8,128)}, u32[]{:S(2)}) %copy-start.2) | copy-done | bytes 32792
  5.2 0.0 copy-start.3
  5.3 0.8 %copy-done.3 = f32[8,8,128]{2,1,0:T(8,128)S(1)} copy-done((f32[8,8,128]{2,1,0:T(8,128)S(1)}, f32[8,8,128]{2,1,0:T(8,128)}, u32[]{:S(2)}) %copy-start.3) | copy-done | bytes 32792
  6.0 0.0 copy-start.4
  6.0 0.8 %copy-done.4 = f32[8,8,128]{2,1,0:T(8,128)S(1)} copy-done((f32[8,8,128]{2,1,0:T(8,128)S(1)}, f32[8,8,128]{2,1,0:T(8,128)}, u32[]{:S(2)}) %copy-start.4) | copy-done | bytes 32792
  6.8 0.0 copy-start.5
  6.8 0.7 %copy-done.5 = f32[24,128]{1,0:T(8,128)S(1)} copy-done((f32[24,128]{1,0:T(8,128)S(1)}, f32[24,128]{1,0:T(8,128)}, u32[]{:S(2)}) %copy-start.5) | copy-done | bytes 12312
  7.5 0.0 copy-start.6
  7.5 0.7 %copy-done.6 = f32[24,128]{1,0:T(8,128)S(1)} copy-done((f32[24,128]{1,0:T(8,128)S(1)}, f32[24,128]{1,0:T(8,128)}, u32[]{:S(2)}) %copy-start.6) | copy-done | bytes 12312
  8.2 57.6 %shard_map.95 = (f32[8,8,128]{2,1,0:T(8,128)S(1)}, f32[8,8,128]{2,1,0:T(8,128)S(1)}) custom-call(f32[8,8,128]{2,1,0:T(8,128)S(1)} %copy-done.1, f32[8,8,128]{2,1,0:T(8,128)S(1)} %copy-done.2, f32[8,8,128]{2,1,0:T(8,128)S(1)} %copy-done.3, f32[8,8,128]{2,1,0:T(8,128)S(1)} %copy-done.4, bf16[24,6,128,128]{3,2,1,0:T(8,128)(2,1)S(1)} %copy-done, ...), custom_call_target="tpu_custom_call" | custom-call | tf_op jit(solution)/shard_map/pallas_call | solution.py:352
  65.8 0.6 copy.13
  66.4 0.6 copy.14
Async XLA Ops:
  1.4 2.3 %copy-start = (bf16[24,6,128,128]{3,2,1,0:T(8,128)(2,1)S(1)}, bf16[24,6,128,128]{3,2,1,0:T(8,128)(2,1)}, u32[]{:S(2)}) copy-start(bf16[24,6,128,128]{3,2,1,0:T(8,128)(2,1)} %blocks_hbm.1) | copy-start | bytes 14155780
  3.7 0.8 %copy-start.1 = (f32[8,8,128]{2,1,0:T(8,128)S(1)}, f32[8,8,128]{2,1,0:T(8,128)}, u32[]{:S(2)}) copy-start(f32[8,8,128]{2,1,0:T(8,128)} %act_hbm.1) | copy-start | bytes 98308
  4.5 0.8 %copy-start.2 = (f32[8,8,128]{2,1,0:T(8,128)S(1)}, f32[8,8,128]{2,1,0:T(8,128)}, u32[]{:S(2)}) copy-start(f32[8,8,128]{2,1,0:T(8,128)} %ana_hbm.1) | copy-start | bytes 98308
  5.2 0.8 %copy-start.3 = (f32[8,8,128]{2,1,0:T(8,128)S(1)}, f32[8,8,128]{2,1,0:T(8,128)}, u32[]{:S(2)}) copy-start(f32[8,8,128]{2,1,0:T(8,128)} %mr_hbm.1) | copy-start | bytes 98308
  6.0 0.8 %copy-start.4 = (f32[8,8,128]{2,1,0:T(8,128)S(1)}, f32[8,8,128]{2,1,0:T(8,128)}, u32[]{:S(2)}) copy-start(f32[8,8,128]{2,1,0:T(8,128)} %sens_hbm.1) | copy-start | bytes 98308
  6.8 0.7 %copy-start.5 = (f32[24,128]{1,0:T(8,128)S(1)}, f32[24,128]{1,0:T(8,128)}, u32[]{:S(2)}) copy-start(f32[24,128]{1,0:T(8,128)} %counts_hbm.1) | copy-start | bytes 36868
  7.5 0.7 %copy-start.6 = (f32[24,128]{1,0:T(8,128)S(1)}, f32[24,128]{1,0:T(8,128)}, u32[]{:S(2)}) copy-start(f32[24,128]{1,0:T(8,128)} %back_hbm.1) | copy-start | bytes 36868

commit v2 on v1

--- a/solution.py
+++ b/solution.py
@@ -22,6 +22,7 @@
 NGX, NGY = 16, 16
 SLABS = 2 * NGX
 TILES, K, LORT, BRICK = 24, 6, 128, 128
+TOGETHER = 12
 KP = 8
 ENTRIES = TILES * KP
 ENTRIES_PAD = 256
@@ -45,6 +46,9 @@
 OFFSETS = offsets()
 INDEX = {p: i for i, p in enumerate(OFFSETS)}
 NEAR_FIRST = OFFSETS[::-1]
+
+
+HALOS = ((-1, 0), (1, 0), (0, -1), (0, 1), (1, -1), (-1, 1))
 
 
 def encode(x):
@@ -86,7 +90,7 @@
     u_ref, v_ref, mr_ref, sens_ref, blk, ids_ref, counts_ref, back_ref,
     gather_ref, scatter_ref, full, picked, expect, ratio, back_terms, own_part,
     send_b, recv_b, send_h, recv_h, strip,
-    load_sem, a_send, a_recv, b_send, b_recv, h_send, h_recv, c_send, c_recv,
+    load_sem, a_send, a_recv, b_send, b_recv, h_send, h_recv, c_send, c_recv, across_sem,
 ):
     gx = lax.axis_index("gx")
     gy = lax.axis_index("gy")
@@ -103,11 +107,19 @@
         return (other // 2, around(gy + dg, NGY), lax.rem(other, 2))
 
     barrier = pltpu.get_barrier_semaphore()
+    first_slab, last_slab = slab == 0, slab == SLABS - 1
+    first_gy, last_gy = gy == 0, gy == NGY - 1
     side = 2 * sub - 1
+    across = (neighbour(side, 0), neighbour(side, -side))
+    before_next = jnp.logical_and(sub == 1, jnp.logical_not(last_slab))
+    after_last = jnp.logical_and(sub == 0, jnp.logical_not(first_slab))
     for a, b in OFFSETS:
         pl.semaphore_signal(barrier, inc=1, device_id=peer(a, b), device_id_type=MESH)
-    pl.semaphore_signal(barrier, inc=1, device_id=neighbour(side, 0), device_id_type=MESH)
-    pl.semaphore_signal(barrier, inc=1, device_id=neighbour(side, -side), device_id_type=MESH)
+
+    @pl.when(before_next)
+    def _():
+        for device in across:
+            pl.semaphore_signal(barrier, inc=1, device_id=device, device_id_type=MESH)
 
     mine = pl.ds(sub * 4, 4)
     loads = [
@@ -149,16 +161,33 @@
             send_h[phase, 4, f, 0:1, :] = ref[3, 0:1, :]
             send_h[phase, 5, f, 0:1, :] = ref[0, 7:8, :]
 
-    def share_halo(phase):
+    def halo_copies(phase):
         copies = []
-        for i, (ds, dg) in enumerate(((-1, 0), (1, 0), (0, -1), (0, 1), (1, -1), (-1, 1))):
+        for i, (ds, dg) in enumerate(HALOS):
             copies.append(pltpu.make_async_remote_copy(
                 src_ref=send_h.at[phase, i], dst_ref=recv_h.at[phase, i],
                 send_sem=h_send.at[phase, i], recv_sem=h_recv.at[phase, i],
                 device_id=neighbour(ds, dg), device_id_type=MESH))
-        for copy in copies:
-            copy.start()
         return copies
+
+    def goes(i):
+        ds = HALOS[i][0]
+        return None if ds == 0 else jnp.logical_not(last_slab if ds > 0 else first_slab)
+
+    def comes(i):
+        ds = HALOS[i][0]
+        return None if ds == 0 else jnp.logical_not(first_slab if ds > 0 else last_slab)
+
+    def only_if(condition, act):
+        if condition is None:
+            act()
+        else:
+            pl.when(condition)(act)
+
+    def start_halo(copies, condition=None):
+        for i, copy in enumerate(copies):
+            terms = [c for c in (condition, goes(i)) if c is not None]
+            only_if(functools.reduce(jnp.logical_and, terms) if terms else None, copy.start)
 
     def gather_bricks(phase, copies):
         total = None
@@ -174,10 +203,9 @@
         return jnp.where(row_id == k, values, 0.0).astype(BF16)
 
     def project(step, carry):
-        for sub_step in range(4):
-            t = step * 4 + sub_step
+        for inner in range(TOGETHER):
+            t = step * TOGETHER + inner
             x = picked[t]
-            total = None
             lhs = jnp.concatenate([only_row(x, k) for k in range(K)], axis=1)
             rhs = jnp.concatenate([blk[t, k] for k in range(K)], axis=1)
             total = dot(lhs, rhs, NT)
@@ -185,8 +213,8 @@
         return carry
 
     def backproject(step, carry):
-        for sub_step in range(4):
-            t = step * 4 + sub_step
+        for inner in range(TOGETHER):
+            t = step * TOGETHER + inner
             r = jnp.broadcast_to(ratio[pl.ds(t, 1), :], (8, LORT))
             lhs = jnp.concatenate([only_row(r, k) for k in range(K)], axis=1)
             back_terms[t] = dot(lhs, blk[t].reshape(K * LORT, BRICK), NN)
@@ -222,12 +250,9 @@
             total = total + decode(recv_b[phase, i])
         return total.reshape(4, 8, BRICK)
 
-    first_slab, last_slab = slab == 0, slab == SLABS - 1
-    first_gy, last_gy = gy == 0, gy == NGY - 1
-
     def prior(phase, copies):
-        for copy in copies:
-            copy.wait_recv()
+        for i, copy in enumerate(copies):
+            only_if(comes(i), copy.wait_recv)
 
         def layers(f, ref):
             return [recv_h[phase, 1, f]] + [ref[x] for x in range(4)] + [recv_h[phase, 0, f]]
@@ -273,17 +298,18 @@
         return result
 
     loads[2].wait()
-    ids = ids_ref[...]
-    lane6 = lax.broadcasted_iota(jnp.int32, (TILES, KP, K), 2)
-    k_of = lax.broadcasted_iota(jnp.int32, (TILES, KP, K), 1)
-    spread = jnp.where(lane6 == k_of, jnp.broadcast_to(ids.reshape(TILES, 1, K), (TILES, KP, K)) + 1, 0)
-    column = jnp.sum(spread.astype(F32), axis=2, keepdims=True) - 1.0
-    column = column.astype(jnp.int32)
-    entry = (lax.broadcasted_iota(jnp.int32, (TILES, KP, ENTRIES_PAD), 0) * KP
-             + lax.broadcasted_iota(jnp.int32, (TILES, KP, ENTRIES_PAD), 1))
+    entry_t = lax.broadcasted_iota(jnp.int32, (TILES, KP, ENTRIES_PAD), 0)
+    entry_k = lax.broadcasted_iota(jnp.int32, (TILES, KP, ENTRIES_PAD), 1)
     lanes = lax.broadcasted_iota(jnp.int32, (TILES, KP, ENTRIES_PAD), 2)
-    as_row = jnp.where(entry == lanes, column + 1, 0).astype(F32)
+    by_tile = jnp.concatenate([ids_ref[...], jnp.zeros((KP - K, TILES), jnp.int32)], axis=0).astype(F32)
+    tile_lane = lax.broadcasted_iota(jnp.int32, (TILES, KP, TILES), 2)
+    tile_of = lax.broadcasted_iota(jnp.int32, (TILES, KP, TILES), 0)
+    k_of = lax.broadcasted_iota(jnp.int32, (TILES, KP, TILES), 1)
+    chosen = jnp.logical_and(tile_lane == tile_of, k_of < K)
+    column = jnp.sum(jnp.where(chosen, by_tile[None] + 1.0, 0.0), axis=2, keepdims=True)
+    as_row = jnp.where(entry_t * KP + entry_k == lanes, column, 0.0)
     as_row = jnp.sum(jnp.sum(as_row, axis=0), axis=0, keepdims=True).astype(jnp.int32) - 1
+    column = column.astype(jnp.int32) - 1
     bricks = lax.broadcasted_iota(jnp.int32, (QUAD, ENTRIES_PAD), 0)
     for a in range(NCX):
         came_from = around(cx - a, NCX) * QUAD
@@ -295,69 +321,97 @@
     loads[0].wait()
     loads[1].wait()
     full[0, 0, own_rows, :] = u_ref[...].reshape(HALF, BRICK).astype(BF16)
-    pack_halo(0)
-
-    pl.semaphore_wait(barrier, len(OFFSETS) + 2)
-
-    pending = []
+
+    @pl.when(jnp.logical_not(after_last))
+    def _():
+        pl.semaphore_wait(barrier, len(OFFSETS))
+
+    @pl.when(after_last)
+    def _():
+        pl.semaphore_wait(barrier, len(OFFSETS) + len(across))
+        for device in across:
+            pl.semaphore_signal(across_sem, inc=1, device_id=device, device_id_type=MESH)
+
+    def swap(i, out):
+        copy = pltpu.make_async_remote_copy(
+            src_ref=out.at[mine], dst_ref=out.at[mine],
+            send_sem=c_send.at[i], recv_sem=c_recv.at[i], device_id=(gx, gy, 1 - sub), device_id_type=MESH)
+        copy.start()
+        return copy
+
+    pending, halos = [], []
     for phase in range(ITERS):
         shared = share(phase)
-        halo = share_halo(phase)
-        pending += shared + halo
+        pack_halo(phase)
+        halo = halo_copies(phase)
+        if phase == 0:
+            start_halo(halo, jnp.logical_not(before_next))
+        else:
+            start_halo(halo)
         if phase == 0:
             for i in (3, 4, 5, 6, 7):
                 loads[i].wait()
         gather_bricks(phase, shared)
-        lax.fori_loop(0, TILES // 4, project, 0)
+        if phase == 0:
+            @pl.when(before_next)
+            def _():
+                pl.semaphore_wait(across_sem, len(across))
+
+            start_halo(halo, before_next)
+        lax.fori_loop(0, TILES // TOGETHER, project, 0)
         ratio[...] = 1.0 - counts_ref[...] / (expect[...] + back_ref[...])
-        lax.fori_loop(0, TILES // 4, backproject, 0)
+        lax.fori_loop(0, TILES // TOGETHER, backproject, 0)
         sent = scatter_and_send(phase)
-        pending += sent
+        pending += shared + sent
+        halos += halo
         prior_u, prior_v = prior(phase, halo)
-        gradient = summed_gradient(phase, sent)
         last = phase == ITERS - 1
+        step = [u_ref[x] / sens_ref[x] for x in range(4)]
         for x in range(4):
-            u, v = u_ref[x], v_ref[x]
-            new_u = jnp.maximum(u - u / sens_ref[x] * (gradient[x] + BETA * prior_u[x]), FLOOR)
+            v = v_ref[x]
             new_v = v - TAU * (v - mr_ref[x] + BETA * prior_v[x])
             if last:
-                u_out[sub * 4 + x] = new_u
                 v_out[sub * 4 + x] = new_v
             else:
+                v_ref[x] = new_v
+        if last:
+            swaps = [swap(1, v_out)]
+        gradient = summed_gradient(phase, sent)
+        for x in range(4):
+            new_u = jnp.maximum(u_ref[x] - step[x] * (gradient[x] + BETA * prior_u[x]), FLOOR)
+            if last:
+                u_out[sub * 4 + x] = new_u
+            else:
                 u_ref[x] = new_u
-                v_ref[x] = new_v
         if not last:
             full[phase + 1, 0, own_rows, :] = u_ref[...].reshape(HALF, BRICK).astype(BF16)
-            pack_halo(phase + 1)
-
-    partner = (gx, gy, 1 - sub)
-    for i, out in enumerate((u_out, v_out)):
-        copy = pltpu.make_async_remote_copy(
-            src_ref=out.at[mine], dst_ref=out.at[mine],
-            send_sem=c_send.at[i], recv_sem=c_recv.at[i], device_id=partner, device_id_type=MESH)
-        copy.start()
-        pending.append(copy)
-    pending[-1].wait_recv()
-    pending[-2].wait_recv()
+
+    swaps.append(swap(0, u_out))
+    for copy in swaps:
+        copy.wait_recv()
+    pending += swaps
     for copy in pending:
         copy.wait_send()
+    for i, copy in enumerate(halos):
+        only_if(goes(i % len(HALOS)), copy.wait_send)
 
 
 def local(activity, anatomy, mr_data, sensitivity, blocks, brick_ids, counts, background):
     n = len(OFFSETS)
-    any_space = pl.BlockSpec(memory_space=pl.ANY)
+    hbm = pl.BlockSpec(memory_space=pltpu.HBM)
     vmem = pl.BlockSpec(memory_space=pltpu.VMEM)
     half = (4, 8, BRICK)
     dma = pltpu.SemaphoreType.DMA
+    operands = (activity, anatomy, mr_data, sensitivity, blocks, brick_ids.T, counts, background)
     return pl.pallas_call(
         kernel,
         out_shape=(jax.ShapeDtypeStruct(activity.shape, F32), jax.ShapeDtypeStruct(anatomy.shape, F32)),
-        in_specs=[any_space] * 8,
+        in_specs=[hbm] * 8,
         out_specs=(vmem, vmem),
         scratch_shapes=[
             pltpu.VMEM(half, F32), pltpu.VMEM(half, F32), pltpu.VMEM(half, F32), pltpu.VMEM(half, F32),
             pltpu.VMEM(blocks.shape, BF16),
-            pltpu.VMEM(brick_ids.shape, jnp.int32),
+            pltpu.VMEM((K, TILES), jnp.int32),
             pltpu.VMEM(counts.shape, F32), pltpu.VMEM(background.shape, F32),
             pltpu.VMEM((NCX, ENTRIES, QUAD), BF16),
             pltpu.VMEM((NCX, QUAD, ENTRIES_PAD), BF16),
@@ -373,11 +427,11 @@
             pltpu.VMEM((ITERS, 6, 2, 8, BRICK), F32),
             pltpu.VMEM((2, 8, BRICK), F32),
             dma((8,)), dma((ITERS, n)), dma((ITERS, n)), dma((ITERS, n)), dma((ITERS, n)),
-            dma((ITERS, 6)), dma((ITERS, 6)), dma((2,)), dma((2,)),
+            dma((ITERS, 6)), dma((ITERS, 6)), dma((2,)), dma((2,)), pltpu.SemaphoreType.REGULAR,
         ],
         compiler_params=pltpu.CompilerParams(
-            collective_id=0, has_side_effects=True, vmem_limit_bytes=24 * 1024 * 1024),
-    )(activity, anatomy, mr_data, sensitivity, blocks, brick_ids, counts, background)
+            collective_id=0, has_side_effects=True, vmem_limit_bytes=32 * 1024 * 1024),
+    )(*[pltpu.with_memory_space_constraint(x, pltpu.HBM) for x in operands])
 
 
 def solution(mesh):

time: 67.6 us -> 54.5 us (0.81)
  the two profiles are of different devices: /device:TPU:192 before, /device:TPU:64 now
where the time goes in v2:
time: 54.5 us; the launch traced here: 54.4 us
  Pallas kernels  52.5 us (96%)
  local copies, waits for them, and re-layouts  1.23 us (2%)
  between operations  0.64 us (1%)
    pallas_call x1, Pallas kernels, local(): pl.pallas_call(kernel, out_shape=(jax.ShapeDtypeStruct(activity.shape, F3...  52.5 us
    unnamed x2, local copies, waits for them, and re-layouts  1.23 us

profile of v2, /device:TPU:64, one launch (start us, length us, event | category | flops | bytes accessed | tf_op | source)
XLA Modules:
  0.0 54.4 jit_solution(2956118167861489275)
XLA Ops:
  0.6 52.5 %shard_map.95 = (f32[8,8,128]{2,1,0:T(8,128)S(1)}, f32[8,8,128]{2,1,0:T(8,128)S(1)}) custom-call(f32[8,8,128]{2,1,0:T(8,128)} %act_hbm.1, f32[8,8,128]{2,1,0:T(8,128)} %ana_hbm.1, f32[8,8,128]{2,1,0:T(8,128)} %mr_hbm.1, f32[8,8,128]{2,1,0:T(8,128)} %sens_hbm.1, bf16[24,6,128,128]{3,2,1,0:T(8,128)(2,1)} %blocks_hbm.1, s32[6,24]{1,0:T(8,128)} %bitcast.1, ...), custom_call_target="tpu_custom_call" | custom-call | tf_op jit(solution)/shard_map/pallas_call | solution.py:406
  53.1 0.6 %copy.12 = f32[8,8,128]{2,1,0:T(8,128)} copy(f32[8,8,128]{2,1,0:T(8,128)S(1)} %get-tuple-element.4) | data formatting | bytes 65536
  53.7 0.6 %copy.13 = f32[8,8,128]{2,1,0:T(8,128)} copy(f32[8,8,128]{2,1,0:T(8,128)S(1)} %get-tuple-element.5) | data formatting | bytes 65536

commit v3 on v2

--- a/solution.py
+++ b/solution.py
@@ -44,8 +44,6 @@
 
 
 OFFSETS = offsets()
-INDEX = {p: i for i, p in enumerate(OFFSETS)}
-NEAR_FIRST = OFFSETS[::-1]
 
 
 HALOS = ((-1, 0), (1, 0), (0, -1), (0, 1), (1, -1), (-1, 1))
@@ -140,16 +138,15 @@
     lane_id = lax.broadcasted_iota(jnp.int32, (8, BRICK), 1)
 
     def share(phase):
-        copies = []
         for a, b in OFFSETS:
-            i = INDEX[a, b]
-            copies.append(pltpu.make_async_remote_copy(
+            pltpu.make_async_remote_copy(
                 src_ref=full.at[phase, 0, own_rows], dst_ref=full.at[phase, a, own_rows],
-                send_sem=a_send.at[phase, i], recv_sem=a_recv.at[phase, i],
-                device_id=peer(a, b), device_id_type=MESH))
-        for copy in copies:
-            copy.start()
-        return copies
+                send_sem=a_send.at[phase, a], recv_sem=a_recv.at[phase, a],
+                device_id=peer(a, b), device_id_type=MESH).start()
+
+    def await_group(ref, a, sem):
+        part = ref.at[pl.ds(0, ref.shape[0] * (NCY - 1) // NCY)] if a == 0 else ref
+        pltpu.make_async_copy(part, part, sem).wait()
 
     def pack_halo(phase):
         for f, ref in enumerate((u_ref, v_ref)):
@@ -189,12 +186,10 @@
             terms = [c for c in (condition, goes(i)) if c is not None]
             only_if(functools.reduce(jnp.logical_and, terms) if terms else None, copy.start)
 
-    def gather_bricks(phase, copies):
+    def gather_bricks(phase):
         total = None
         for a in (0, 1, 3, 2):
-            for b in range(NCY):
-                if (a, b) != (0, 0):
-                    copies[INDEX[a, b]].wait_recv()
+            await_group(full.at[phase, a], a, a_recv.at[phase, a])
             part = dot(gather_ref[a], full[phase, a], NN)
             total = part if total is None else total + part
         picked[...] = total.reshape(TILES, KP, BRICK)
@@ -224,7 +219,6 @@
         terms = back_terms[...].reshape(ENTRIES_PAD, BRICK)
         high = terms.astype(BF16)
         low = (terms - high.astype(F32)).astype(BF16)
-        copies = [None] * len(OFFSETS)
         for a in (2, 1, 3, 0):
             part = dot(scatter_ref[a], high, NN) + dot(scatter_ref[a], low, NN)
             send_b[phase, a] = encode(part)
@@ -233,22 +227,24 @@
             for x, b in OFFSETS:
                 if x != a:
                     continue
-                i = INDEX[a, b]
                 rows = pl.ds(pl.multiple_of(lax.rem(cy + b, NCY) * HALF, HALF), HALF)
-                copies[i] = pltpu.make_async_remote_copy(
-                    src_ref=send_b.at[phase, a, rows], dst_ref=recv_b.at[phase, i],
-                    send_sem=b_send.at[phase, i], recv_sem=b_recv.at[phase, i],
-                    device_id=peer(a, b), device_id_type=MESH)
-                copies[i].start()
-        return copies
-
-    def summed_gradient(phase, copies):
+                slot = b - 1 if a == 0 else b
+                pltpu.make_async_remote_copy(
+                    src_ref=send_b.at[phase, a, rows], dst_ref=recv_b.at[phase, a, slot],
+                    send_sem=b_send.at[phase, a], recv_sem=b_recv.at[phase, a],
+                    device_id=peer(a, b), device_id_type=MESH).start()
+
+    def summed_gradient(phase):
         total = own_part[own_rows, :]
-        for p in NEAR_FIRST:
-            i = INDEX[p]
-            copies[i].wait_recv()
-            total = total + decode(recv_b[phase, i])
+        for a in (0, 1, 3, 2):
+            await_group(recv_b.at[phase, a], a, b_recv.at[phase, a])
+            for slot in range(NCY - 1 if a == 0 else NCY):
+                total = total + decode(recv_b[phase, a, slot])
         return total.reshape(4, 8, BRICK)
+
+    def await_sends(sent, phase, sems):
+        for a in range(NCX):
+            await_group(sent.at[phase, a], a, sems.at[phase, a])
 
     def prior(phase, copies):
         for i, copy in enumerate(copies):
@@ -339,9 +335,9 @@
         copy.start()
         return copy
 
-    pending, halos = [], []
+    halos = []
     for phase in range(ITERS):
-        shared = share(phase)
+        share(phase)
         pack_halo(phase)
         halo = halo_copies(phase)
         if phase == 0:
@@ -351,7 +347,7 @@
         if phase == 0:
             for i in (3, 4, 5, 6, 7):
                 loads[i].wait()
-        gather_bricks(phase, shared)
+        gather_bricks(phase)
         if phase == 0:
             @pl.when(before_next)
             def _():
@@ -361,8 +357,8 @@
         lax.fori_loop(0, TILES // TOGETHER, project, 0)
         ratio[...] = 1.0 - counts_ref[...] / (expect[...] + back_ref[...])
         lax.fori_loop(0, TILES // TOGETHER, backproject, 0)
-        sent = scatter_and_send(phase)
-        pending += shared + sent
+        scatter_and_send(phase)
+        await_sends(full, phase, a_send)
         halos += halo
         prior_u, prior_v = prior(phase, halo)
         last = phase == ITERS - 1
@@ -376,7 +372,7 @@
                 v_ref[x] = new_v
         if last:
             swaps = [swap(1, v_out)]
-        gradient = summed_gradient(phase, sent)
+        gradient = summed_gradient(phase)
         for x in range(4):
             new_u = jnp.maximum(u_ref[x] - step[x] * (gradient[x] + BETA * prior_u[x]), FLOOR)
             if last:
@@ -387,17 +383,16 @@
             full[phase + 1, 0, own_rows, :] = u_ref[...].reshape(HALF, BRICK).astype(BF16)
 
     swaps.append(swap(0, u_out))
-    for copy in swaps:
-        copy.wait_recv()
-    pending += swaps
-    for copy in pending:
-        copy.wait_send()
+    for phase in range(ITERS):
+        await_sends(send_b, phase, b_send)
     for i, copy in enumerate(halos):
         only_if(goes(i % len(HALOS)), copy.wait_send)
+    for copy in swaps:
+        copy.wait()
 
 
 def local(activity, anatomy, mr_data, sensitivity, blocks, brick_ids, counts, background):
-    n = len(OFFSETS)
+    groups = (ITERS, NCX)
     hbm = pl.BlockSpec(memory_space=pltpu.HBM)
     vmem = pl.BlockSpec(memory_space=pltpu.VMEM)
     half = (4, 8, BRICK)
@@ -422,11 +417,11 @@
             pltpu.VMEM((ENTRIES_PAD // KP, KP, BRICK), F32),
             pltpu.VMEM((QUAD, BRICK), F32),
             pltpu.VMEM((ITERS, NCX, QUAD, BRICK), jnp.int16),
-            pltpu.VMEM((ITERS, n, HALF, BRICK), jnp.int16),
+            pltpu.VMEM((ITERS, NCX, NCY, HALF, BRICK), jnp.int16),
             pltpu.VMEM((ITERS, 6, 2, 8, BRICK), F32),
             pltpu.VMEM((ITERS, 6, 2, 8, BRICK), F32),
             pltpu.VMEM((2, 8, BRICK), F32),
-            dma((8,)), dma((ITERS, n)), dma((ITERS, n)), dma((ITERS, n)), dma((ITERS, n)),
+            dma((8,)), dma(groups), dma(groups), dma(groups), dma(groups),
             dma((ITERS, 6)), dma((ITERS, 6)), dma((2,)), dma((2,)), pltpu.SemaphoreType.REGULAR,
         ],
         compiler_params=pltpu.CompilerParams(

time: 54.5 us -> 52.3 us (0.960)
  Pallas kernels: 52.5 us -> 50.3 us
    pallas_call x1, Pallas kernels: 52.5 us -> 50.3 us  [local(): pl.pallas_call(kernel, out_shape=(jax.ShapeDtypeStruct(activity.shape, F3...]
where the time goes in v3:
time: 52.3 us; the launch traced here: 52.2 us
  Pallas kernels  50.3 us (96%)
  local copies, waits for them, and re-layouts  1.23 us (2%)
  between operations  0.64 us (1%)
    pallas_call x1, Pallas kernels, local(): pl.pallas_call(kernel, out_shape=(jax.ShapeDtypeStruct(activity.shape, F3...  50.3 us
    unnamed x2, local copies, waits for them, and re-layouts  1.23 us

profile of v3, /device:TPU:64, one launch (start us, length us, event | category | flops | bytes accessed | tf_op | source)
XLA Modules:
  0.0 52.2 jit_solution(18182709353718796388)
XLA Ops:
  0.6 50.3 %shard_map.95 = (f32[8,8,128]{2,1,0:T(8,128)S(1)}, f32[8,8,128]{2,1,0:T(8,128)S(1)}) custom-call(f32[8,8,128]{2,1,0:T(8,128)} %act_hbm.1, f32[8,8,128]{2,1,0:T(8,128)} %ana_hbm.1, f32[8,8,128]{2,1,0:T(8,128)} %mr_hbm.1, f32[8,8,128]{2,1,0:T(8,128)} %sens_hbm.1, bf16[24,6,128,128]{3,2,1,0:T(8,128)(2,1)} %blocks_hbm.1, s32[6,24]{1,0:T(8,128)} %bitcast.1, ...), custom_call_target="tpu_custom_call" | custom-call | tf_op jit(solution)/shard_map/pallas_call | solution.py:401
  50.9 0.6 %copy.12 = f32[8,8,128]{2,1,0:T(8,128)} copy(f32[8,8,128]{2,1,0:T(8,128)S(1)} %get-tuple-element.4) | data formatting | bytes 65536
  51.6 0.6 %copy.13 = f32[8,8,128]{2,1,0:T(8,128)} copy(f32[8,8,128]{2,1,0:T(8,128)S(1)} %get-tuple-element.5) | data formatting | bytes 65536

commit v4 on v3

--- a/solution.py
+++ b/solution.py
@@ -22,7 +22,7 @@
 NGX, NGY = 16, 16
 SLABS = 2 * NGX
 TILES, K, LORT, BRICK = 24, 6, 128, 128
-TOGETHER = 12
+TOGETHER = 24
 KP = 8
 ENTRIES = TILES * KP
 ENTRIES_PAD = 256
@@ -87,7 +87,7 @@
     u_out, v_out,
     u_ref, v_ref, mr_ref, sens_ref, blk, ids_ref, counts_ref, back_ref,
     gather_ref, scatter_ref, full, picked, expect, ratio, back_terms, own_part,
-    send_b, recv_b, send_h, recv_h, strip,
+    send_b, recv_b, send_h, recv_h, strip, act_all,
     load_sem, a_send, a_recv, b_send, b_recv, h_send, h_recv, c_send, c_recv, across_sem,
 ):
     gx = lax.axis_index("gx")
@@ -129,11 +129,13 @@
         pltpu.make_async_copy(back_hbm, back_ref, load_sem.at[5]),
         pltpu.make_async_copy(mr_hbm.at[mine], mr_ref, load_sem.at[6]),
         pltpu.make_async_copy(sens_hbm.at[mine], sens_ref, load_sem.at[7]),
+        pltpu.make_async_copy(act_hbm, act_all, load_sem.at[8]),
     ]
     for load in loads:
         load.start()
 
     own_rows = pl.ds(pl.multiple_of(cy * HALF, HALF), HALF)
+    pair_rows = pl.ds(pl.multiple_of(cy // 2 * (2 * HALF), 2 * HALF), 2 * HALF)
     row_id = lax.broadcasted_iota(jnp.int32, (8, BRICK), 0)
     lane_id = lax.broadcasted_iota(jnp.int32, (8, BRICK), 1)
 
@@ -144,8 +146,17 @@
                 send_sem=a_send.at[phase, a], recv_sem=a_recv.at[phase, a],
                 device_id=peer(a, b), device_id_type=MESH).start()
 
-    def await_group(ref, a, sem):
-        part = ref.at[pl.ds(0, ref.shape[0] * (NCY - 1) // NCY)] if a == 0 else ref
+    def share_first(phase):
+        for d in (3, 2, 1, 0):
+            for a in (2, 1, 3, 0):
+                if (a, d) != (0, 0):
+                    pltpu.make_async_remote_copy(
+                        src_ref=full.at[phase, 0, pair_rows], dst_ref=full.at[phase, a, pair_rows],
+                        send_sem=a_send.at[phase, a], recv_sem=a_recv.at[phase, a],
+                        device_id=peer(a, NCY + side * d), device_id_type=MESH).start()
+
+    def await_group(ref, a, sem, own=1):
+        part = ref.at[pl.ds(0, ref.shape[0] * (NCY - own) // NCY)] if a == 0 else ref
         pltpu.make_async_copy(part, part, sem).wait()
 
     def pack_halo(phase):
@@ -189,7 +200,7 @@
     def gather_bricks(phase):
         total = None
         for a in (0, 1, 3, 2):
-            await_group(full.at[phase, a], a, a_recv.at[phase, a])
+            await_group(full.at[phase, a], a, a_recv.at[phase, a], own=2 if phase == 0 else 1)
             part = dot(gather_ref[a], full[phase, a], NN)
             total = part if total is None else total + part
         picked[...] = total.reshape(TILES, KP, BRICK)
@@ -197,22 +208,28 @@
     def only_row(values, k):
         return jnp.where(row_id == k, values, 0.0).astype(BF16)
 
+    def spread_rows(values):
+        rows = [jnp.concatenate([jnp.where(row_id == k, x, 0.0) for k in range(K)], axis=1) for x in values]
+        return jnp.concatenate(rows, axis=0).astype(BF16)
+
     def project(step, carry):
-        for inner in range(TOGETHER):
+        for inner in range(0, TOGETHER, 2):
             t = step * TOGETHER + inner
-            x = picked[t]
-            lhs = jnp.concatenate([only_row(x, k) for k in range(K)], axis=1)
-            rhs = jnp.concatenate([blk[t, k] for k in range(K)], axis=1)
-            total = dot(lhs, rhs, NT)
-            expect[pl.ds(t, 1), :] = jnp.sum(total, axis=0, keepdims=True)
+            rows = [jnp.concatenate([blk[t + i, k] for k in range(K)], axis=1) for i in range(2)]
+            total = dot(spread_rows([picked[t], picked[t + 1]]), jnp.concatenate(rows, axis=0), NT)
+            for i in range(2):
+                part = total[8 * i:8 * i + 8, LORT * i:LORT * i + LORT]
+                expect[pl.ds(t + i, 1), :] = jnp.sum(part, axis=0, keepdims=True)
         return carry
 
     def backproject(step, carry):
-        for inner in range(TOGETHER):
+        for inner in range(0, TOGETHER, 2):
             t = step * TOGETHER + inner
-            r = jnp.broadcast_to(ratio[pl.ds(t, 1), :], (8, LORT))
-            lhs = jnp.concatenate([only_row(r, k) for k in range(K)], axis=1)
-            back_terms[t] = dot(lhs, blk[t].reshape(K * LORT, BRICK), NN)
+            r = [jnp.broadcast_to(ratio[pl.ds(t + i, 1), :], (8, LORT)) for i in range(2)]
+            columns = [blk[t + i].reshape(K * LORT, BRICK) for i in range(2)]
+            total = dot(spread_rows(r), jnp.concatenate(columns, axis=1), NN)
+            for i in range(2):
+                back_terms[t + i] = total[8 * i:8 * i + 8, BRICK * i:BRICK * i + BRICK]
         return carry
 
     def scatter_and_send(phase):
@@ -242,9 +259,9 @@
                 total = total + decode(recv_b[phase, a, slot])
         return total.reshape(4, 8, BRICK)
 
-    def await_sends(sent, phase, sems):
+    def await_sends(sent, phase, sems, own=1):
         for a in range(NCX):
-            await_group(sent.at[phase, a], a, sems.at[phase, a])
+            await_group(sent.at[phase, a], a, sems.at[phase, a], own)
 
     def prior(phase, copies):
         for i, copy in enumerate(copies):
@@ -316,7 +333,8 @@
     send_h[...] = jnp.zeros_like(send_h)
     loads[0].wait()
     loads[1].wait()
-    full[0, 0, own_rows, :] = u_ref[...].reshape(HALF, BRICK).astype(BF16)
+    loads[8].wait()
+    full[0, 0, pair_rows, :] = act_all[...].reshape(2 * HALF, BRICK).astype(BF16)
 
     @pl.when(jnp.logical_not(after_last))
     def _():
@@ -337,7 +355,10 @@
 
     halos = []
     for phase in range(ITERS):
-        share(phase)
+        if phase == 0:
+            share_first(phase)
+        else:
+            share(phase)
         pack_halo(phase)
         halo = halo_copies(phase)
         if phase == 0:
@@ -358,7 +379,7 @@
         ratio[...] = 1.0 - counts_ref[...] / (expect[...] + back_ref[...])
         lax.fori_loop(0, TILES // TOGETHER, backproject, 0)
         scatter_and_send(phase)
-        await_sends(full, phase, a_send)
+        await_sends(full, phase, a_send, own=2 if phase == 0 else 1)
         halos += halo
         prior_u, prior_v = prior(phase, halo)
         last = phase == ITERS - 1
@@ -421,7 +442,8 @@
             pltpu.VMEM((ITERS, 6, 2, 8, BRICK), F32),
             pltpu.VMEM((ITERS, 6, 2, 8, BRICK), F32),
             pltpu.VMEM((2, 8, BRICK), F32),
-            dma((8,)), dma(groups), dma(groups), dma(groups), dma(groups),
+            pltpu.VMEM(activity.shape, F32),
+            dma((9,)), dma(groups), dma(groups), dma(groups), dma(groups),
             dma((ITERS, 6)), dma((ITERS, 6)), dma((2,)), dma((2,)), pltpu.SemaphoreType.REGULAR,
         ],
         compiler_params=pltpu.CompilerParams(

time: 52.3 us -> 50.4 us (0.964)
  the two profiles are of different devices: /device:TPU:64 before, /device:TPU:192 now
where the time goes in v4:
time: 50.4 us; the launch traced here: 50.3 us
  Pallas kernels  48.4 us (96%)
  local copies, waits for them, and re-layouts  1.23 us (2%)
  between operations  0.64 us (1%)
    pallas_call x1, Pallas kernels, local(): pl.pallas_call(kernel, out_shape=(jax.ShapeDtypeStruct(activity.shape, F3...  48.4 us
    unnamed x2, local copies, waits for them, and re-layouts  1.23 us

profile of v4, /device:TPU:192, one launch (start us, length us, event | category | flops | bytes accessed | tf_op | source)
XLA Modules:
  0.0 50.3 jit_solution(18128550465065196906)
XLA Ops:
  0.6 48.4 %shard_map.95 = (f32[8,8,128]{2,1,0:T(8,128)S(1)}, f32[8,8,128]{2,1,0:T(8,128)S(1)}) custom-call(f32[8,8,128]{2,1,0:T(8,128)} %act_hbm.1, f32[8,8,128]{2,1,0:T(8,128)} %ana_hbm.1, f32[8,8,128]{2,1,0:T(8,128)} %mr_hbm.1, f32[8,8,128]{2,1,0:T(8,128)} %sens_hbm.1, bf16[24,6,128,128]{3,2,1,0:T(8,128)(2,1)} %blocks_hbm.1, s32[6,24]{1,0:T(8,128)} %bitcast.1, ...), custom_call_target="tpu_custom_call" | custom-call | tf_op jit(solution)/shard_map/pallas_call | solution.py:422
  49.1 0.6 %copy.12 = f32[8,8,128]{2,1,0:T(8,128)} copy(f32[8,8,128]{2,1,0:T(8,128)S(1)} %get-tuple-element.4) | data formatting | bytes 65536
  49.7 0.6 %copy.13 = f32[8,8,128]{2,1,0:T(8,128)} copy(f32[8,8,128]{2,1,0:T(8,128)S(1)} %get-tuple-element.5) | data formatting | bytes 65536

commit v5 on v4

--- a/solution.py
+++ b/solution.py
@@ -236,20 +236,22 @@
         terms = back_terms[...].reshape(ENTRIES_PAD, BRICK)
         high = terms.astype(BF16)
         low = (terms - high.astype(F32)).astype(BF16)
-        for a in (2, 1, 3, 0):
-            part = dot(scatter_ref[a], high, NN) + dot(scatter_ref[a], low, NN)
-            send_b[phase, a] = encode(part)
-            if a == 0:
-                own_part[...] = part
-            for x, b in OFFSETS:
-                if x != a:
-                    continue
-                rows = pl.ds(pl.multiple_of(lax.rem(cy + b, NCY) * HALF, HALF), HALF)
-                slot = b - 1 if a == 0 else b
-                pltpu.make_async_remote_copy(
-                    src_ref=send_b.at[phase, a, rows], dst_ref=recv_b.at[phase, a, slot],
-                    send_sem=b_send.at[phase, a], recv_sem=b_recv.at[phase, a],
-                    device_id=peer(a, b), device_id_type=MESH).start()
+        for group in ((2,), (1, 3, 0)):
+            for a in group:
+                part = dot(scatter_ref[a], high, NN) + dot(scatter_ref[a], low, NN)
+                send_b[phase, a] = encode(part)
+                if a == 0:
+                    own_part[...] = part
+            for a in group:
+                for x, b in OFFSETS:
+                    if x != a:
+                        continue
+                    rows = pl.ds(pl.multiple_of(lax.rem(cy + b, NCY) * HALF, HALF), HALF)
+                    slot = b - 1 if a == 0 else b
+                    pltpu.make_async_remote_copy(
+                        src_ref=send_b.at[phase, a, rows], dst_ref=recv_b.at[phase, a, slot],
+                        send_sem=b_send.at[phase, a], recv_sem=b_recv.at[phase, a],
+                        device_id=peer(a, b), device_id_type=MESH).start()
 
     def summed_gradient(phase):
         total = own_part[own_rows, :]

time: 50.4 us -> 50.3 us (level)
  the two profiles are of different devices: /device:TPU:192 before, /device:TPU:64 now
where the time goes in v5:
time: 50.3 us; the launch traced here: 49.7 us
  Pallas kernels  47.8 us (95%)
  local copies, waits for them, and re-layouts  1.23 us (2%)
  between operations  0.64 us (1%)
    pallas_call x1, Pallas kernels, local(): pl.pallas_call(kernel, out_shape=(jax.ShapeDtypeStruct(activity.shape, F3...  47.8 us
    unnamed x2, local copies, waits for them, and re-layouts  1.23 us

profile of v5, /device:TPU:64, one launch (start us, length us, event | category | flops | bytes accessed | tf_op | source)
XLA Modules:
  0.0 49.7 jit_solution(1499930427396718848)
XLA Ops:
  0.6 47.8 %shard_map.95 = (f32[8,8,128]{2,1,0:T(8,128)S(1)}, f32[8,8,128]{2,1,0:T(8,128)S(1)}) custom-call(f32[8,8,128]{2,1,0:T(8,128)} %act_hbm.1, f32[8,8,128]{2,1,0:T(8,128)} %ana_hbm.1, f32[8,8,128]{2,1,0:T(8,128)} %mr_hbm.1, f32[8,8,128]{2,1,0:T(8,128)} %sens_hbm.1, bf16[24,6,128,128]{3,2,1,0:T(8,128)(2,1)} %blocks_hbm.1, s32[6,24]{1,0:T(8,128)} %bitcast.1, ...), custom_call_target="tpu_custom_call" | custom-call | tf_op jit(solution)/shard_map/pallas_call | solution.py:424
  48.4 0.6 %copy.12 = f32[8,8,128]{2,1,0:T(8,128)} copy(f32[8,8,128]{2,1,0:T(8,128)S(1)} %get-tuple-element.4) | data formatting | bytes 65536
  49.0 0.6 %copy.13 = f32[8,8,128]{2,1,0:T(8,128)} copy(f32[8,8,128]{2,1,0:T(8,128)S(1)} %get-tuple-element.5) | data formatting | bytes 65536
